TPU v7x, 32 devices: a whole 2x2x4 slice. The times are simulated.
32 devices in a mesh: parts: 2 (over x), brick: 16 (over z, y, core).
Axes of the slice: x: 2, y: 2, z: 4, core: 2. Of those that a mesh axis runs over, the one named last changes fastest.
Arguments:
- tokens: bfloat16 [4096, 1024], P(('parts', 'brick')), parts along dimension 0, may hold values from -6 to 6
- norm_gain: float32 [1024], replicated, may hold values from 0.5 to 2
- in_projection: bfloat16 [1024, 3072], replicated
- out_projection: bfloat16 [1024, 1024], replicated, may hold values from -0.1875 to 0.1875
- out_cotangent: bfloat16 [4096, 1024], P(('parts', 'brick')), parts along dimension 0, may hold values from -6 to 6
Outputs:
- layer_output: bfloat16 [4096, 1024], P(('parts', 'brick')), parts along dimension 0
- grad_tokens: bfloat16 [4096, 1024], P(('parts', 'brick')), parts along dimension 0
- grad_in_projection: float32 [2048, 3072], P(('parts', 'brick')), parts along dimension 0
- grad_out_projection: float32 [2048, 1024], P('parts', 'brick'), parts along dimension 0
- grad_norm_gain: float32 [2048], P(('parts', 'brick')), parts along dimension 0
There are 2 independent parts, one for each index of `parts`. A program takes and returns all parts, laid end to end along the dimension named above; an argument that names none is the same for every part. Nothing has to cross between parts.
All inputs are finite; a program needn't handle non-finite values.
Results may differ from a plain program's by a relative error of at most 0.011.
Values may be sent and summed in bfloat16 or wider, within the bound.
A program may use at most 256 MiB of HBM per device.

v0:
```python
import math

import jax
import jax.numpy as jnp
from jax import lax
from jax.sharding import PartitionSpec as P

D = 1024
HEADS = 16
HEAD_DIM = 64
BRICK_A = 4
BRICK_B = 4
BRICK_C = 8
WINDOW = 256


norm_epsilon = 1e-05


def score_rows(query_rows, key_rows):
    return jnp.einsum(
        "qd,kd->qk", query_rows, key_rows, preferred_element_type=jnp.float32
    ) * HEAD_DIM ** (-0.5)


def forward_item(triple):
    window_len = triple.shape[1]
    block_len = math.gcd(window_len, 512)
    key_rows, value_rows = (triple[1], triple[2])
    query_blocks = triple[0].reshape(window_len // block_len, block_len, HEAD_DIM)

    def forward_one_block(query_rows):
        scores = score_rows(query_rows, key_rows)
        maxima = jnp.max(scores, axis=-1)
        shifted = jnp.exp(scores - maxima[:, None])
        totals = jnp.sum(shifted, axis=-1)
        soft_rounded = (shifted / totals[:, None]).astype(jnp.bfloat16)
        attended = jnp.dot(soft_rounded, value_rows, preferred_element_type=jnp.float32).astype(
            jnp.bfloat16
        )
        return (attended, maxima, totals)

    attended, maxima, totals = lax.map(forward_one_block, query_blocks)
    return (
        attended.reshape(window_len, HEAD_DIM),
        maxima.reshape(window_len),
        totals.reshape(window_len),
    )


def forward_items(piece):
    item_len = piece.shape[1]
    class_len = piece.shape[3] // HEAD_DIM
    groups = class_len // WINDOW
    item_stack = piece.reshape(item_len, 3, groups, WINDOW, HEAD_DIM).transpose(0, 2, 1, 3, 4)
    item_stack = item_stack.reshape(item_len * groups, 3, WINDOW, HEAD_DIM)
    attended, maxima, totals = lax.map(forward_item, item_stack)
    return (
        attended.reshape(1, item_len, class_len * HEAD_DIM),
        maxima.reshape(1, item_len, class_len),
        totals.reshape(1, item_len, class_len),
        piece,
    )


def backward_item(inputs):
    triple, d_output, maxima, totals = inputs
    window_len = triple.shape[1]
    block_len = math.gcd(window_len, 512)
    block_count = window_len // block_len
    key_rows, value_rows = (triple[1], triple[2])
    sliced = (
        triple[0].reshape(block_count, block_len, HEAD_DIM),
        d_output.reshape(block_count, block_len, HEAD_DIM),
        maxima.reshape(block_count, block_len),
        totals.reshape(block_count, block_len),
    )

    def backward_one_block(accumulated, pieces):
        query_rows, d_rows, max_rows, total_rows = pieces
        scores = score_rows(query_rows, key_rows)
        shifted = jnp.exp(scores - jnp.max(scores, axis=-1, keepdims=True))
        soft_weights = shifted / jnp.sum(shifted, axis=-1, keepdims=True)
        soft_rounded = soft_weights.astype(jnp.bfloat16)
        d_soft = jnp.einsum("qd,kd->qk", d_rows, value_rows, preferred_element_type=jnp.float32)
        d_scores = soft_weights * (d_soft - jnp.sum(soft_weights * d_soft, axis=-1, keepdims=True))
        d_scaled = (d_scores * HEAD_DIM ** (-0.5)).astype(jnp.bfloat16)
        d_queries = jnp.dot(d_scaled, key_rows, preferred_element_type=jnp.float32).astype(
            jnp.bfloat16
        )
        key_total = accumulated[0] + jnp.einsum(
            "qk,qd->kd", d_scaled, query_rows, preferred_element_type=jnp.float32
        )
        value_total = accumulated[1] + jnp.einsum(
            "qk,qd->kd", soft_rounded, d_rows, preferred_element_type=jnp.float32
        )
        return ((key_total, value_total), d_queries)

    zeros_acc = jnp.zeros((window_len, HEAD_DIM), jnp.float32)
    accumulated, d_queries = lax.scan(backward_one_block, (zeros_acc, zeros_acc), sliced)
    return jnp.stack(
        [
            d_queries.reshape(window_len, HEAD_DIM),
            accumulated[0].astype(jnp.bfloat16),
            accumulated[1].astype(jnp.bfloat16),
        ]
    )


def per_device(tokens, norm_gain, in_projection, out_projection, out_cotangent):
    brick_count = lax.axis_size("brick")
    tok_count = tokens.shape[0]
    tok_class = tok_count // 8
    item_count = 8 * HEADS // brick_count
    widened = tokens.astype(jnp.float32)
    centre = widened - jnp.mean(widened, axis=-1, keepdims=True)
    inverse_dev = lax.rsqrt(jnp.mean(centre * centre, axis=-1, keepdims=True) + norm_epsilon)
    standard = centre * inverse_dev
    normed = (standard * norm_gain).astype(jnp.bfloat16)
    projected = jnp.dot(normed, in_projection, preferred_element_type=jnp.float32).astype(
        jnp.bfloat16
    )
    shaped = projected.reshape(
        BRICK_A // 2, 2, BRICK_B // 2, 2, BRICK_C // 2, 2, 3, HEADS, HEAD_DIM
    )
    outgoing = shaped.transpose(1, 3, 5, 7, 6, 0, 2, 4, 8).reshape(
        brick_count, item_count, 3, tok_class * HEAD_DIM
    )
    attended_items, row_maxima, row_totals, kept_items = forward_items(
        lax.all_to_all(outgoing, "brick", split_axis=0, concat_axis=3, tiled=True)
    )
    returned_items = lax.all_to_all(
        attended_items, "brick", split_axis=2, concat_axis=0, tiled=True
    )
    attended = returned_items.reshape(
        2, 2, 2, HEADS, BRICK_A // 2, BRICK_B // 2, BRICK_C // 2, HEAD_DIM
    )
    attended = attended.transpose(4, 0, 5, 1, 6, 2, 3, 7).reshape(tok_count, D)
    layer_output = jnp.dot(attended, out_projection, preferred_element_type=jnp.float32).astype(
        jnp.bfloat16
    )
    d_attended = jnp.einsum(
        "tf,df->td", out_cotangent, out_projection, preferred_element_type=jnp.float32
    ).astype(jnp.bfloat16)
    out_term = jnp.einsum("td,tf->df", attended, out_cotangent, preferred_element_type=jnp.float32)
    grad_out_projection = lax.psum_scatter(out_term, "brick", scatter_dimension=1, tiled=True)
    d_shaped = d_attended.reshape(
        BRICK_A // 2, 2, BRICK_B // 2, 2, BRICK_C // 2, 2, HEADS, HEAD_DIM
    )
    d_outgoing = d_shaped.transpose(1, 3, 5, 6, 0, 2, 4, 7).reshape(
        brick_count, item_count, tok_class * HEAD_DIM
    )
    d_items = lax.all_to_all(d_outgoing, "brick", split_axis=0, concat_axis=2, tiled=True)
    class_len = d_items.shape[2] // HEAD_DIM
    groups = class_len // WINDOW
    item_stack = kept_items.reshape(item_count, 3, groups, WINDOW, HEAD_DIM).transpose(
        0, 2, 1, 3, 4
    )
    item_stack = item_stack.reshape(item_count * groups, 3, WINDOW, HEAD_DIM)
    item_grads = lax.map(
        backward_item,
        (
            item_stack,
            d_items.reshape(item_count * groups, WINDOW, HEAD_DIM),
            row_maxima.reshape(item_count * groups, WINDOW),
            row_totals.reshape(item_count * groups, WINDOW),
        ),
    )
    grad_outgoing = item_grads.reshape(item_count, groups, 3, WINDOW, HEAD_DIM).transpose(
        0, 2, 1, 3, 4
    )
    grad_outgoing = grad_outgoing.reshape(1, item_count, 3, class_len * HEAD_DIM)
    grad_returned = lax.all_to_all(grad_outgoing, "brick", split_axis=3, concat_axis=0, tiled=True)
    d_projected = grad_returned.reshape(
        2, 2, 2, HEADS, 3, BRICK_A // 2, BRICK_B // 2, BRICK_C // 2, HEAD_DIM
    )
    d_projected = d_projected.transpose(5, 0, 6, 1, 7, 2, 4, 3, 8).reshape(tok_count, 3 * D)
    d_normed = jnp.einsum(
        "tf,df->td", d_projected, in_projection, preferred_element_type=jnp.float32
    )
    gain_term = jnp.sum(d_normed * standard, axis=0)
    weighted = d_normed * norm_gain
    mean_one = jnp.mean(weighted, axis=-1, keepdims=True)
    mean_two = jnp.mean(weighted * standard, axis=-1, keepdims=True)
    grad_tokens = (inverse_dev * (weighted - mean_one - standard * mean_two)).astype(jnp.bfloat16)
    in_term = jnp.einsum("td,tf->df", normed, d_projected, preferred_element_type=jnp.float32)
    grad_in_projection, grad_norm_gain = (
        lax.psum_scatter(in_term, "brick", scatter_dimension=0, tiled=True),
        lax.psum_scatter(gain_term, "brick", scatter_dimension=0, tiled=True),
    )
    return (layer_output, grad_tokens, grad_in_projection, grad_out_projection, grad_norm_gain)


def solution(mesh):
    placed = (P(("parts", "brick"), None), P(), P(), P(), P(("parts", "brick"), None))
    return jax.shard_map(
        per_device,
        mesh=mesh,
        in_specs=placed,
        out_specs=(
            P(("parts", "brick"), None),
            P(("parts", "brick"), None),
            P(("parts", "brick"), None),
            P("parts", "brick"),
            P(("parts", "brick")),
        ),
        check_vma=False,
    )
```

profile of v0, /device:TPU:0, one launch (start us, length us, event | category | flops | bytes accessed | tf_op | source)
XLA Modules:
  0.0 548.0 jit_solution(17481336225304496887)
XLA Ops:
  9.6 4.0 convolution_convert_fusion.4
  13.6 1.9 reshape.84
  15.5 3.4 copy.64
  18.8 3.0 reshape.85
  22.8 7.4 %all-to-all-start = ((bf16[16,8,3,1024]{3,1,2,0:T(8,128)(2,1)}), bf16[16,8,3,1024]{3,1,2,0:T(8,128)(2,1)S(1)}, u32[]{:S(2)}, u32[]{:S(2)}) async-start(bf16[16,8,3,1024]{3,1,2,0:T(8,128)(2,1)} %copy.42), calls=%async_computation | async-start | bytes 1572864 | tf_op jit(solution)/shard_map/all_to_all | solution.py:130
  34.2 2.1 reshape.90
  36.3 12.6 %all-to-all-done = bf16[16,8,3,1024]{3,1,2,0:T(8,128)(2,1)S(1)} async-done(((bf16[16,8,3,1024]{3,1,2,0:T(8,128)(2,1)}), bf16[16,8,3,1024]{3,1,2,0:T(8,128)(2,1)S(1)}, u32[]{:S(2)}, u32[]{:S(2)}) %all-to-all-start) | async-done | bytes 786464 | tf_op jit(solution)/shard_map/all_to_all | solution.py:130
  48.9 5.5 %all-to-all-start.2 = ((bf16[16,8,1024]{2,1,0:T(8,128)(2,1)}), bf16[16,8,1024]{2,1,0:T(8,128)(2,1)S(1)}, u32[]{:S(2)}, u32[]{:S(2)}) async-start(bf16[16,8,1024]{2,1,0:T(8,128)(2,1)} %reshape.90), calls=%async_computation.2 | async-start | bytes 524288 | tf_op jit(solution)/shard_map/all_to_all | solution.py:153
  55.8 3.2 reshape_transpose_reshape.7
  59.0 17.8 %while.16 = (s32[]{:T(128)}, bf16[8,256,64]{1,2,0:T(8,128)(2,1)S(1)}, bf16[8,3,256,64]{3,2,1,0:T(8,128)(2,1)}, s32[]{:T(128)}, s32[]{:T(128)}, /*index=5*/s32[]{}, s32[]{}) while((s32[]{:T(128)}, bf16[8,256,64]{1,2,0:T(8,128)(2,1)S(1)}, bf16[8,3,256,64]{3,2,1,0:T(8,128)(2,1)}, s32[]{:T(128)}, s32[]{:T(128)}, /*index=5*/s32[]{}, s32[]{}) %tuple.63), condition=%wide.region_5.0_spmd, body=%wide.region_2.5_spmd.sunk | while | flops 17251844 | bytes 1024109 | solution.py:57
  77.5 12.7 %copy.45 = bf16[1,8,16384]{1,0,2:T(2,128)(2,1)} copy(bf16[1,8,16384]{2,1,0:T(8,128)(2,1)S(1)} %reshape.86) | data formatting | bytes 524288 | tf_op jit(solution)/shard_map/reshape | solution.py:59
  90.7 90.8 %reduce = bf16[16384,8]{1,0:T(8,128)(2,1)} reduce(bf16[16384,1,8]{2,1,0:T(2,128)(2,1)} %bitcast.149, bf16[]{:T(256)} %broadcast.57), dimensions={1}, to_apply=%bitcast.81.reduce_sub_computation | reduce | bytes 524290
  181.5 6.4 %reshape.95 = bf16[16,2,4096]{2,1,0:T(2,128)(2,1)} reshape(bf16[16384,8]{1,0:T(8,128)(2,1)} %reduce) | data formatting | bytes 524288
  187.9 6.0 %all-to-all-start.1 = ((bf16[16,2,4096]{2,1,0:T(2,128)(2,1)}), bf16[16,2,4096]{2,1,0:T(2,128)(2,1)S(1)}, u32[]{:S(2)}, u32[]{:S(2)}) async-start(bf16[16,2,4096]{2,1,0:T(2,128)(2,1)} %reshape.95), calls=%async_computation.1 | async-start | bytes 524288 | tf_op jit(solution)/shard_map/all_to_all | solution.py:132
  195.3 8.7 %all-to-all-done.1 = bf16[16,2,4096]{2,1,0:T(2,128)(2,1)S(1)} async-done(((bf16[16,2,4096]{2,1,0:T(2,128)(2,1)}), bf16[16,2,4096]{2,1,0:T(2,128)(2,1)S(1)}, u32[]{:S(2)}, u32[]{:S(2)}) %all-to-all-start.1) | async-done | bytes 262176 | tf_op jit(solution)/shard_map/all_to_all | solution.py:132
  204.0 12.3 %reshape.96 = bf16[16384,1,8]{2,1,0:T(2,128)(2,1)} reshape(bf16[16,2,4096]{2,1,0:T(2,128)(2,1)S(1)} %all-to-all-done.1) | data formatting | bytes 524288
  216.3 14.8 %copy.46 = bf16[1,8,16384]{2,1,0:T(8,128)(2,1)S(1)} copy(bf16[1,8,16384]{1,0,2:T(2,128)(2,1)} %bitcast.150) | data formatting | bytes 524288 | tf_op jit(solution)/shard_map/all_to_all | solution.py:132
  232.2 3.6 fusion.43
  236.1 49.4 %while.17 = (s32[]{:T(128)}, bf16[8,3,256,64]{2,3,1,0:T(8,128)(2,1)}, bf16[8,3,256,64]{3,2,1,0:T(8,128)(2,1)}, bf16[8,256,64]{2,1,0:T(8,128)(2,1)}, s32[]{:T(128)}, /*index=5*/s32[]{:T(128)}, s32[]{}, s32[]{}) while((s32[]{:T(128)}, bf16[8,3,256,64]{2,3,1,0:T(8,128)(2,1)}, bf16[8,3,256,64]{3,2,1,0:T(8,128)(2,1)}, ...), condition=%wide.region_10.11_spmd, body=%wide.region_6.10_spmd.sunk | while | flops 43400452 | bytes 2996361 | solution.py:160
  285.5 27.9 %copy.56 = bf16[8,3,256,64]{0,1,3,2:T(4,128)(2,1)} copy(bf16[8,3,256,64]{2,3,1,0:T(8,128)(2,1)} %get-tuple-element.84) | data formatting | bytes 1572864 | tf_op jit(solution)/shard_map/reshape;transpose;reshape | solution.py:172
  313.4 18.2 %reshape.97 = bf16[16,2,12288]{2,1,0:T(2,128)(2,1)S(1)} reshape(bf16[16384,1,3,8]{3,2,1,0:T(4,128)(2,1)} %bitcast.147) | data formatting | bytes 1572864
  331.6 23.6 %all_to_all.60 = bf16[16,2,12288]{2,1,0:T(2,128)(2,1)} all-to-all(bf16[16,2,12288]{2,1,0:T(2,128)(2,1)S(1)} %reshape.97), channel_id=1, replica_groups=mesh['parts'=2,'brick'=16] {'brick'}, dimensions={0} | all-to-all | bytes 1572864 | tf_op jit(solution)/shard_map/all_to_all | solution.py:173
  355.2 17.6 %reshape.98 = bf16[16384,1,3,8]{3,2,1,0:T(4,128)(2,1)} reshape(bf16[16,2,12288]{2,1,0:T(2,128)(2,1)} %all_to_all.60) | data formatting | bytes 1572864
  372.8 20.7 %copy.58 = bf16[1,8,3,16,1024]{4,1,3,2,0:T(8,128)(2,1)S(1)} copy(bf16[1,8,3,16,1024]{1,2,4,3,0:T(4,128)(2,1)} %bitcast.148) | data formatting | bytes 1572864 | tf_op jit(solution)/shard_map/all_to_all | solution.py:173
  393.6 1.9 reshape.92
  395.5 3.0 copy.55
  398.5 2.3 reshape.93
  400.8 6.5 %fusion.38 = f32[1024,3072]{1,0:T(8,128)} fusion(bf16[128,3072]{1,0:T(8,128)(2,1)S(1)} %reshape.93, bf16[128,1024]{1,0:T(8,128)(2,1)S(1)} %copy-done.1, f32[1024]{0:T(1024)S(1)} %copy-done.3, f32[128]{0:T(128)S(1)} %add_rsqrt_fusion, f32[128]{0:T(128)S(1)} %broadcast_multiply_fusion.2), kind=kOutput, calls=%fused_computation.68 | convolution fusion | flops 805961728 | bytes 13636608 | tf_op jit(solution)/shard_map/td,tf->df/dot_general | solution.py:186
  410.3 6.4 %fusion.36 = (f32[1024]{0:T(1024)S(1)}, f32[128]{0:T(128)S(1)}, f32[128]{0:T(128)S(1)}, f32[128,1024]{1,0:T(8,128)}) fusion(bf16[128,1024]{1,0:T(8,128)(2,1)S(1)} %copy-done.1, f32[128]{0:T(128)S(1)} %add_rsqrt_fusion, f32[128]{0:T(128)S(1)} %broadcast_multiply_fusion.2, f32[1024]{0:T(1024)S(1)} %copy-done.3, bf16[128,3072]{1,0:T(8,128)(2,1)S(1)} %reshape.93, ...), kind=kOutput, calls=%fused_computation.59 | convolution fusion | flops 806484736 | bytes 7874560 | tf_op jit(solution)/shard_map/tf,df->td/dot_general | solution.py:178
  416.7 31.7 %all-reduce = f32[1024]{0:T(1024)S(1)} all-reduce(f32[1024]{0:T(1024)S(1)} %get-tuple-element.85), channel_id=4, replica_groups=mesh['parts'=2,'brick'=16] {'brick'}, use_global_device_ids=true, to_apply=%region_16.17.clone | all-reduce | flops 1024 | bytes 8192
  448.9 2.0 fusion.35
  450.9 90.3 %reduce-scatter.3.cloned.1.call-done = f32[64,3072]{1,0:T(8,128)} async-done(((f32[1024,3072]{1,0:T(8,128)}), f32[64,3072]{1,0:T(8,128)}) %reduce-scatter.3.cloned.1.call-update) | async-done | bytes 786448 | tf_op jit(solution)/shard_map/reduce_scatter | solution.py:188
  (131 shorter events, 82.3 us)
Async XLA Ops:
  7.2 23.1 %copy-start = (bf16[1024,1024]{1,0:T(8,128)(2,1)S(1)}, bf16[1024,1024]{1,0:T(8,128)(2,1)}, u32[]{:S(2)}) copy-start(bf16[1024,1024]{1,0:T(8,128)(2,1)} %param.12) | copy-start | bytes 6291460
  21.9 8.4 %copy-start.2 = (bf16[128,1024]{1,0:T(8,128)(2,1)S(1)}, bf16[128,1024]{1,0:T(8,128)(2,1)}, u32[]{:S(2)}) copy-start(bf16[128,1024]{1,0:T(8,128)(2,1)} %param.13) | copy-start | bytes 786436
  22.8 26.1 %all-to-all-start = ((bf16[16,8,3,1024]{3,1,2,0:T(8,128)(2,1)}), bf16[16,8,3,1024]{3,1,2,0:T(8,128)(2,1)S(1)}, u32[]{:S(2)}, u32[]{:S(2)}) async-start(bf16[16,8,3,1024]{3,1,2,0:T(8,128)(2,1)} %copy.42), calls=%async_computation | async-start | bytes 1572864 | tf_op jit(solution)/shard_map/all_to_all | solution.py:130
  48.9 139.0 %all-to-all-start.2 = ((bf16[16,8,1024]{2,1,0:T(8,128)(2,1)}), bf16[16,8,1024]{2,1,0:T(8,128)(2,1)S(1)}, u32[]{:S(2)}, u32[]{:S(2)}) async-start(bf16[16,8,1024]{2,1,0:T(8,128)(2,1)} %reshape.90), calls=%async_computation.2 | async-start | bytes 524288 | tf_op jit(solution)/shard_map/all_to_all | solution.py:153
  54.4 4.5 copy-start.4
  187.9 16.1 %all-to-all-start.1 = ((bf16[16,2,4096]{2,1,0:T(2,128)(2,1)}), bf16[16,2,4096]{2,1,0:T(2,128)(2,1)S(1)}, u32[]{:S(2)}, u32[]{:S(2)}) async-start(bf16[16,2,4096]{2,1,0:T(2,128)(2,1)} %reshape.95), calls=%async_computation.1 | async-start | bytes 524288 | tf_op jit(solution)/shard_map/all_to_all | solution.py:132
  194.0 256.9 %reduce-scatter.5.cloned.1.call-start = ((), (), s32[]{:S(2)}) async-start(), calls=%async_computation.7 | async-start | bytes 4456448 | tf_op jit(solution)/shard_map/reduce_scatter | solution.py:146
  235.8 305.3 %reduce-scatter.3.cloned.1.call-start = ((), (), s32[]{:S(2)}) async-start(), calls=%async_computation.6 | async-start | bytes 13369344 | tf_op jit(solution)/shard_map/reduce_scatter | solution.py:188
  395.5 5.3 copy-start.1
  395.5 5.3 copy-start.3
  407.3 0.7 copy-start.5
Sparse Core Ops, SparseCore 0:
  236.0 71.0 reduce-scatter.4
  407.4 133.7 reduce-scatter.2
where the time goes:
time: 553 us; the launch traced here: 548 us
  local copies, waits for them, and re-layouts  162 us (29%)
  waiting for transfers between devices  112 us (20%)
  other arithmetic  102 us (18%)
  matrix products  82.9 us (15%)
  blocking collectives  55.2 us (10%)
  starting transfers between devices  19.2 us (3%)
  between operations  14.9 us (3%)
    unnamed x1, other arithmetic  90.8 us
    reduce_scatter x1, waiting for transfers between devices, per_device(): lax.psum_scatter(in_term, 'brick', scatter_dimension=0, tiled=True)  90.3 us
    unnamed x20, local copies, waits for them, and re-layouts  57 us
    unnamed x1, blocking collectives  31.7 us
    another operation x1, local copies, waits for them, and re-layouts, per_device(): grad_outgoing.reshape(1, item_count, 3, class_len * HEAD_DIM)  27.9 us
    all_to_all x1, blocking collectives, per_device(): lax.all_to_all(grad_outgoing, 'brick', split_axis=3, concat_axis=0, tiled...  23.6 us
    all_to_all x1, local copies, waits for them, and re-layouts, per_device(): lax.all_to_all(grad_outgoing, 'brick', split_axis=3, concat_axis=0, tiled...  20.7 us
    dot_general x16, matrix products, score_rows(): jnp.einsum('qd,kd->qk', query_rows, key_rows, preferred_element_type=jnp....  17.5 us
  transfers between devices with their start and end apart: 5, of which 3 were waited for; matrix products, arithmetic and copies ran while one was open for 54% of the time, Pallas kernels for 0%

commit v1 on v0

v1 whole, which is shorter than its diff:
```python
import functools

import jax
import jax.numpy as jnp
import numpy as np
from jax import lax
from jax.experimental import pallas as pl
from jax.experimental.pallas import tpu as pltpu
from jax.sharding import Mesh, PartitionSpec as P

D = 1024
HEADS = 16
HEAD_DIM = 64
GROUP = 16
CLASSES = 8
BLOCK = 16
HALF = 512
SCALE = HEAD_DIM ** (-0.5)
EPS = 1e-05
BF = jnp.bfloat16
F32 = jnp.float32
MESH = pl.DeviceIdType.MESH
MB = 1024 * 1024


def dot(a, b, ca, cb):
    return lax.dot_general(a, b, (((ca,), (cb,)), ((), ())), preferred_element_type=F32)


def permutation(transposed):
    shape = (128, 128)
    r = lax.broadcasted_iota(jnp.int32, shape, 1 if transposed else 0)
    s = lax.broadcasted_iota(jnp.int32, shape, 0 if transposed else 1)
    a = 2 * ((r >> 3) & 1) + ((r >> 6) & 1)
    p = 2 * ((r >> 2) & 1) + ((r >> 5) & 1)
    c = 2 * (r & 3) + ((r >> 4) & 1)
    return jnp.where(s == (a * 4 + p) * 8 + c, 1.0, 0.0).astype(BF)


def place():
    core = lax.axis_index("core")
    chip = lax.axis_index("chip")
    base = (chip // CLASSES) * CLASSES
    mine = (chip - base) * 2 + core
    return core, chip, base, mine


def device(base, local):
    return {"chip": base + local // 2, "core": local % 2}


def enter(base, mine):
    barrier = pltpu.get_barrier_semaphore()

    def greet(j, _):
        pl.semaphore_signal(
            barrier, inc=1, device_id=device(base, lax.rem(mine + j, GROUP)), device_id_type=MESH
        )
        return 0

    lax.fori_loop(1, GROUP, greet, 0)
    pl.semaphore_wait(barrier, GROUP - 1)


def gather_kernel(tok, cot, x, g, ptok, pcot, send, recv, psend, precv):
    core, chip, base, mine = place()
    perm = permutation(False)
    ptok[...] = jnp.dot(perm, tok[...], preferred_element_type=F32).astype(BF)
    pcot[...] = jnp.dot(perm, cot[...], preferred_element_type=F32).astype(BF)
    enter(base, mine)

    def copy(k, src, dst, peer, sender, j):
        rows = pl.ds(pl.multiple_of((peer // 2) * BLOCK, BLOCK), BLOCK)
        cols = pl.ds(pl.multiple_of((peer % 2) * HALF, HALF), HALF)
        landing = pl.ds(pl.multiple_of(sender * BLOCK, BLOCK), BLOCK)
        return pltpu.make_async_remote_copy(
            src_ref=src.at[rows, cols],
            dst_ref=dst.at[landing, cols],
            send_sem=send.at[k, j],
            recv_sem=recv.at[k, j],
            device_id=device(base, peer),
            device_id_type=MESH,
        )

    pairs = ((ptok, x), (pcot, g))
    for k, (src, dst) in enumerate(pairs):

        def start(j, _):
            copy(k, src, dst, lax.rem(mine + j, GROUP), mine, j).start()
            return 0

        lax.fori_loop(1, GROUP, start, 0)
    cols = pl.ds(pl.multiple_of(core * HALF, HALF), HALF)
    own = pl.ds(pl.multiple_of(mine * BLOCK, BLOCK), BLOCK)
    own_class = pl.ds(pl.multiple_of((mine // 2) * BLOCK, BLOCK), BLOCK)
    forwards = []
    for k, (src, dst) in enumerate(pairs):
        dst[own, cols] = src[own_class, cols]

        def finish(j, _):
            c = copy(k, src, dst, lax.rem(mine + j, GROUP), mine, j)
            c.wait_send()
            c.wait_recv()
            return 0

        lax.fori_loop(1, GROUP, finish, 0)
        f = pltpu.make_async_remote_copy(
            src_ref=dst.at[:, cols],
            dst_ref=dst.at[:, cols],
            send_sem=psend.at[k],
            recv_sem=precv.at[k],
            device_id={"core": 1 - core},
            device_id_type=MESH,
        )
        f.start()
        forwards.append(f)
    for f in forwards:
        f.wait_send()
        f.wait_recv()


def vmem():
    return pl.BlockSpec(memory_space=pltpu.VMEM)


def gather(tokens, cot):
    return pl.pallas_call(
        gather_kernel,
        out_shape=[jax.ShapeDtypeStruct((256, D), BF)] * 2,
        in_specs=[vmem()] * 2,
        out_specs=[vmem()] * 2,
        scratch_shapes=[
            pltpu.VMEM((128, D), BF),
            pltpu.VMEM((128, D), BF),
            pltpu.SemaphoreType.DMA((2, GROUP)),
            pltpu.SemaphoreType.DMA((2, GROUP)),
            pltpu.SemaphoreType.DMA((2,)),
            pltpu.SemaphoreType.DMA((2,)),
        ],
        compiler_params=pltpu.CompilerParams(
            collective_id=0, has_side_effects=True, vmem_limit_bytes=16 * MB
        ),
    )(tokens, cot)


def normalise(x):
    wide = x.astype(F32)
    centre = wide - jnp.mean(wide, axis=-1, keepdims=True)
    inverse = lax.rsqrt(jnp.mean(centre * centre, axis=-1, keepdims=True) + EPS)
    return centre * inverse, inverse


def work_kernel(x, g, gain, w_in, w_out, part_out, part_dn, terms, wi, wo, nrm, proj, att, dpr, sem):
    core = lax.axis_index("core")
    cols = pl.multiple_of(core * HALF, HALF)
    copies = [
        pltpu.make_async_copy(w_in.at[:, pl.ds(i * D + cols, HALF)], wi.at[i], sem.at[i])
        for i in range(3)
    ]
    copies.append(pltpu.make_async_copy(w_out.at[pl.ds(cols, HALF), :], wo, sem.at[3]))
    for c in copies:
        c.start()
    standard, _ = normalise(x[...])
    nrm[...] = (standard * gain[...]).astype(BF)
    for i in range(3):
        copies[i].wait()
        proj[i] = dot(nrm[...], wi[i], 1, 0).astype(BF)
    copies[3].wait()
    proj[3] = dot(g[...], wo[...], 1, 1).astype(BF)

    for h in range(HALF // HEAD_DIM):
        at = slice(h * HEAD_DIM, (h + 1) * HEAD_DIM)
        q, k, v, do = (proj[i, :, at] for i in range(4))
        scores = dot(q, k, 1, 1) * SCALE
        shifted = jnp.exp(scores - jnp.max(scores, axis=-1, keepdims=True))
        soft = shifted / jnp.sum(shifted, axis=-1, keepdims=True)
        rounded = soft.astype(BF)
        att[:, at] = dot(rounded, v, 1, 0).astype(BF)
        d_soft = dot(do, v, 1, 1)
        d_scores = soft * (d_soft - jnp.sum(soft * d_soft, axis=-1, keepdims=True))
        d_scaled = (d_scores * SCALE).astype(BF)
        dpr[0, :, at] = dot(d_scaled, k, 1, 0).astype(BF)
        dpr[1, :, at] = dot(d_scaled, q, 0, 0).astype(BF)
        dpr[2, :, at] = dot(rounded, do, 0, 0).astype(BF)

    part_out[...] = dot(att[...], wo[...], 1, 0)
    terms[:, 3 * HALF :] = dot(g[...], att[...], 0, 0).astype(BF)
    for i in range(3):
        terms[:, i * HALF : (i + 1) * HALF] = dot(nrm[...], dpr[i], 0, 0).astype(BF)
    part_dn[...] = (
        dot(dpr[0], wi[0], 1, 1) + dot(dpr[1], wi[1], 1, 1) + dot(dpr[2], wi[2], 1, 1)
    )


def work(x, g, gain, w_in, w_out):
    return pl.pallas_call(
        work_kernel,
        out_shape=[
            jax.ShapeDtypeStruct((256, D), F32),
            jax.ShapeDtypeStruct((256, D), F32),
            jax.ShapeDtypeStruct((D, 4 * HALF), BF),
        ],
        in_specs=[vmem()] * 3 + [pl.BlockSpec(memory_space=pl.ANY)] * 2,
        out_specs=[vmem()] * 3,
        scratch_shapes=[
            pltpu.VMEM((3, D, HALF), BF),
            pltpu.VMEM((HALF, D), BF),
            pltpu.VMEM((256, D), BF),
            pltpu.VMEM((4, 256, HALF), BF),
            pltpu.VMEM((256, HALF), BF),
            pltpu.VMEM((3, 256, HALF), BF),
            pltpu.SemaphoreType.DMA((4,)),
        ],
        compiler_params=pltpu.CompilerParams(vmem_limit_bytes=40 * MB),
    )(x, g, gain, w_in, w_out)


def return_kernel(x, gain, part_out, part_dn, out, grad, oland, dland, oret, dret, oin, din, psend, precv, send, recv):
    core, chip, base, mine = place()
    enter(base, mine)
    theirs = pl.ds(pl.multiple_of((1 - core) * 128, 128), 128)
    ours = pl.ds(pl.multiple_of(core * 128, 128), 128)
    swaps = []
    for k, (src, dst) in enumerate(((part_out, oland), (part_dn, dland))):
        c = pltpu.make_async_remote_copy(
            src_ref=src.at[theirs, :],
            dst_ref=dst,
            send_sem=psend.at[k],
            recv_sem=precv.at[k],
            device_id={"core": 1 - core},
            device_id_type=MESH,
        )
        c.start()
        swaps.append(c)

    def send_back(k, src, dst, j):
        brick = core * 8 + j
        rows = pl.ds(pl.multiple_of(j * BLOCK, BLOCK), BLOCK)
        landing = pl.ds(pl.multiple_of((mine // 2) * BLOCK, BLOCK), BLOCK)
        return pltpu.make_async_remote_copy(
            src_ref=src.at[rows, :],
            dst_ref=dst.at[landing, :],
            send_sem=send.at[k, j],
            recv_sem=recv.at[k, mine // 2],
            device_id=device(base, brick),
            device_id_type=MESH,
        )

    def deliver(k, src, dst):
        own_rows = pl.ds(pl.multiple_of((mine // 2) * BLOCK, BLOCK), BLOCK)
        for j in range(8):
            brick = core * 8 + j

            @pl.when(brick != mine)
            def _():
                send_back(k, src, dst, j).start()

            @pl.when(brick == mine)
            def _():
                dst[own_rows, :] = src[j * BLOCK : (j + 1) * BLOCK, :]

    swaps[0].wait_send()
    swaps[0].wait_recv()
    oret[...] = (part_out[ours, :] + oland[...]).astype(BF)
    deliver(0, oret, oin)
    swaps[1].wait_send()
    swaps[1].wait_recv()
    standard, inverse = normalise(x[ours, :])
    weighted = (part_dn[ours, :] + dland[...]) * gain[...]
    mean_one = jnp.mean(weighted, axis=-1, keepdims=True)
    mean_two = jnp.mean(weighted * standard, axis=-1, keepdims=True)
    dret[...] = (inverse * (weighted - mean_one - standard * mean_two)).astype(BF)
    deliver(1, dret, din)
    home = mine // 8
    inverse_perm = permutation(True)
    for k, (src, dst, result) in enumerate(((oret, oin, out), (dret, din, grad))):
        for j in range(8):

            @pl.when(core * 8 + j != mine)
            def _():
                send_back(k, src, dst, j).wait_send()

            @pl.when(j * 2 + home != mine)
            def _():
                pltpu.make_async_remote_copy(
                    src_ref=src.at[j * BLOCK : (j + 1) * BLOCK, :],
                    dst_ref=dst.at[j * BLOCK : (j + 1) * BLOCK, :],
                    send_sem=send.at[k, j],
                    recv_sem=recv.at[k, j],
                    device_id={"core": 1 - core},
                    device_id_type=MESH,
                ).wait_recv()

        result[...] = jnp.dot(inverse_perm, dst[...], preferred_element_type=F32).astype(BF)


def give_back(x, gain, part_out, part_dn):
    return pl.pallas_call(
        return_kernel,
        out_shape=[jax.ShapeDtypeStruct((128, D), BF)] * 2,
        in_specs=[vmem()] * 4,
        out_specs=[vmem()] * 2,
        scratch_shapes=[
            pltpu.VMEM((128, D), F32),
            pltpu.VMEM((128, D), F32),
            pltpu.VMEM((128, D), BF),
            pltpu.VMEM((128, D), BF),
            pltpu.VMEM((128, D), BF),
            pltpu.VMEM((128, D), BF),
            pltpu.SemaphoreType.DMA((2,)),
            pltpu.SemaphoreType.DMA((2,)),
            pltpu.SemaphoreType.DMA((2, 8)),
            pltpu.SemaphoreType.DMA((2, 8)),
        ],
        compiler_params=pltpu.CompilerParams(
            collective_id=1, has_side_effects=True, vmem_limit_bytes=24 * MB
        ),
    )(x, gain, part_out, part_dn)


def per_device(tokens, norm_gain, in_projection, out_projection, out_cotangent):
    core = lax.axis_index("core")
    chip = lax.axis_index("chip")
    gain = norm_gain.reshape(1, D)
    x, g = gather(tokens, out_cotangent)
    part_out, part_dn, terms = work(x, g, gain, in_projection, out_projection)
    summed = lax.psum_scatter(terms, "chip", scatter_dimension=0, tiled=True)
    layer_output, grad_tokens = give_back(x, gain, part_out, part_dn)
    rows = summed.shape[0] // 2
    theirs = lax.dynamic_slice_in_dim(summed, (1 - core) * rows, rows, 0)
    ours = lax.dynamic_slice_in_dim(summed, core * rows, rows, 0).astype(F32)
    got = lax.ppermute(theirs, "core", [(0, 1), (1, 0)]).astype(F32)
    low = jnp.where(core == 0, ours, got)
    high = jnp.where(core == 0, got, ours)
    both = jnp.stack([low.reshape(rows, 4, HALF), high.reshape(rows, 4, HALF)], axis=2)
    both = both.reshape(rows, 4, D)
    grad_in = both[:, :3].reshape(rows, 3 * D)
    grad_out = both[:, 3].T
    start = (chip * 2 + core) * rows
    w_rows = lax.dynamic_slice_in_dim(in_projection, start, rows, 0).astype(F32)
    my_gain = lax.dynamic_slice_in_dim(norm_gain, start, rows, 0)
    grad_gain = jnp.sum(w_rows * grad_in, axis=-1) / my_gain
    return layer_output, grad_tokens, grad_in, grad_out, grad_gain


def solution(mesh):
    parts, bricks = mesh.devices.shape
    fine = Mesh(mesh.devices.reshape(parts, bricks // 2, 2), ("parts", "chip", "core"))
    every = ("parts", "chip", "core")
    placed = (P(every, None), P(), P(), P(), P(every, None))
    return jax.shard_map(
        per_device,
        mesh=fine,
        in_specs=placed,
        out_specs=(
            P(every, None),
            P(every, None),
            P(every, None),
            P("parts", ("chip", "core")),
            P(every),
        ),
        check_vma=False,
    )
```

time: 553 us -> 165 us (0.30)
  local copies, waits for them, and re-layouts: 162 us -> 11.8 us
  other arithmetic: 102 us -> 3.45 us
  matrix products: 82.9 us -> 0 us
  blocking collectives: 55.2 us -> 0 us
  Pallas kernels: 0 us -> 43.5 us
  waiting for transfers between devices: 112 us -> 90 us
  starting transfers between devices: 19.2 us -> 0.11 us
    unnamed x1 -> x0, other arithmetic: 90.8 us -> none
    dot_general x62 -> x0, matrix products: 82.9 us -> none  [the longest x16 17.5 us: score_rows(): jnp.einsum('qd,kd->qk', query_rows, key_rows, preferred_element_type=jnp....]
    unnamed x20 -> x17, local copies, waits for them, and re-layouts: 57 us -> 7.59 us
    pallas_call x0 -> x3, Pallas kernels: none -> 43.5 us  [the longest x1 18.9 us: gather(): pl.pallas_call(gather_kernel, out_shape=[jax.ShapeDtypeStruct((256, D), B...]
    all_to_all x5 -> x0, local copies, waits for them, and re-layouts: 37.1 us -> none  [the longest x1 20.7 us: per_device(): lax.all_to_all(grad_outgoing, 'brick', split_axis=3, concat_axis=0, tiled...]
    reshape x14 -> x2, local copies, waits for them, and re-layouts: 32.9 us -> 0.97 us  [the longest x1 0.9 us: per_device(): both = both.reshape(rows, 4, D)]
    unnamed x1 -> x0, blocking collectives: 31.7 us -> none
    another operation x2 -> x3, local copies, waits for them, and re-layouts: 31.1 us -> 1.51 us  [per_device(): jnp.stack([low.reshape(rows, 4, HALF), high.reshape(rows, 4, HALF)], axis=2)]
  transfers between devices with their start and end apart: 5 -> 2, of which waited for: 3 -> 1; matrix products, arithmetic and copies ran while one was open for 54% -> 0% of each run, Pallas kernels for 0% -> 9%
where the time goes in v1:
time: 165 us; the launch traced here: 163 us
  waiting for transfers between devices  90 us (55%)
  Pallas kernels  43.5 us (26%)
  between operations  14.2 us (9%)
  local copies, waits for them, and re-layouts  11.8 us (7%)
  other arithmetic  3.45 us (2%)
    reduce_scatter x1, waiting for transfers between devices, per_device(): summed = lax.psum_scatter(terms, 'chip', scatter_dimension=0, tiled=True)  89.9 us
    pallas_call x1, Pallas kernels, gather(): pl.pallas_call(gather_kernel, out_shape=[jax.ShapeDtypeStruct((256, D), B...  18.9 us
    pallas_call x1, Pallas kernels, give_back(): pl.pallas_call(return_kernel, out_shape=[jax.ShapeDtypeStruct((128, D), B...  14.6 us
    pallas_call x1, Pallas kernels, work(): pl.pallas_call(work_kernel, out_shape=[jax.ShapeDtypeStruct((256, D), F32...  10 us
    unnamed x17, local copies, waits for them, and re-layouts  7.59 us
  transfers between devices with their start and end apart: 2, of which 1 were waited for; matrix products, arithmetic and copies ran while one was open for 0% of the time, Pallas kernels for 9%

profile of v1, /device:TPU:0, one launch (start us, length us, event | category | flops | bytes accessed | tf_op | source)
XLA Modules:
  0.0 163.0 jit_solution(1822440016691429627)
XLA Ops:
  7.2 0.0 reduce-scatter.2.cloned.1.call-start
  7.2 0.0 copy-start.2
  7.2 0.9 copy-done.2
  8.2 0.9 copy-done.3
  9.1 18.9 %shard_map.92 = (bf16[256,1024]{1,0:T(8,128)(2,1)S(1)}, bf16[256,1024]{1,0:T(8,128)(2,1)S(1)}) custom-call(bf16[128,1024]{1,0:T(8,128)(2,1)S(1)} %copy-done.2, bf16[128,1024]{1,0:T(8,128)(2,1)S(1)} %copy-done.3), custom_call_target="tpu_custom_call" | custom-call | tf_op jit(solution)/shard_map/pallas_call | solution.py:127
  28.1 0.0 copy-start.1
  28.1 1.6 copy-done.1
  29.7 0.7 copy-done.4
  30.4 10.0 %shard_map.93 = (f32[256,1024]{1,0:T(8,128)S(1)}, f32[256,1024]{1,0:T(8,128)S(1)}, bf16[1024,2048]{1,0:T(8,128)(2,1)S(1)}) custom-call(bf16[256,1024]{1,0:T(8,128)(2,1)S(1)} %get-tuple-element.12.x, bf16[256,1024]{1,0:T(8,128)(2,1)S(1)} %get-tuple-element.13.g, f32[1,1024]{1,0:T(1,128)S(1)} %bitcast.10, bf16[1024,3072]{1,0:T(8,128)(2,1)} %w_in.1, ...), custom_call_target="tpu_custom_call" | custom-call | tf_op jit(solution)/shard_map/pallas_call | solution.py:196
  40.4 0.0 copy-start
  40.4 1.9 %copy-done = bf16[1024,2048]{1,0:T(8,128)(2,1)} copy-done((bf16[1024,2048]{1,0:T(8,128)(2,1)}, bf16[1024,2048]{1,0:T(8,128)(2,1)S(1)}, u32[]{:S(2)}) %copy-start) | copy-done | bytes 4194328
  42.3 0.0 reduce-scatter.2.cloned.1.call-update
  42.4 89.9 %reduce-scatter.2.cloned.1.call-done = bf16[128,2048]{1,0:T(8,128)(2,1)} async-done(((bf16[1024,2048]{1,0:T(8,128)(2,1)}), bf16[128,2048]{1,0:T(8,128)(2,1)}) %reduce-scatter.2.cloned.1.call-update) | async-done | bytes 524304 | tf_op jit(solution)/shard_map/reduce_scatter | solution.py:327
  132.3 1.0 constant_dynamic-slice_fusion
  133.3 0.1 collective-permute-start
  133.4 14.6 %shard_map.94 = (bf16[128,1024]{1,0:T(8,128)(2,1)S(1)}, bf16[128,1024]{1,0:T(8,128)(2,1)S(1)}) custom-call(bf16[256,1024]{1,0:T(8,128)(2,1)S(1)} %get-tuple-element.12.x, f32[1,1024]{1,0:T(1,128)S(1)} %bitcast.11, f32[256,1024]{1,0:T(8,128)S(1)} %get-tuple-element.14.part_out, f32[256,1024]{1,0:T(8,128)S(1)} %get-tuple-element.15.part_dn), custom_call_target="tpu_custom_call" | custom-call | tf_op jit(solution)/shard_map/pallas_call | solution.py:298
  148.0 0.0 collective-permute-done
  148.0 1.1 convert_select_fusion.1
  149.1 0.4 stack_reshape.7
  149.5 0.4 stack_reshape.6
  149.8 0.2 pad_maximum_fusion
  150.1 0.8 copy.11
  150.9 0.9 reshape.20
  151.8 0.1 slice_bitcast_fusion
  151.9 0.7 slice_bitcast_fusion.1
  152.6 0.1 copy.13
  152.7 0.0 copy-start.6
  152.7 1.5 multiply_reduce_fusion
  154.2 0.6 dynamic-slice_divide_fusion
  154.8 0.7 copy.16
  155.5 0.7 copy.17
  156.2 0.0 copy-done.6
  (4 shorter events, 0.0 us)
Async XLA Ops:
  7.2 125.2 %reduce-scatter.2.cloned.1.call-start = ((), (), s32[]{:S(2)}) async-start(), calls=%async_computation.1 | async-start | bytes 4718592 | tf_op jit(solution)/shard_map/reduce_scatter | solution.py:327
  7.2 1.0 copy-start.2
  8.2 0.9 copy-start.3
  28.1 1.6 copy-start.1
  29.7 0.7 copy-start.4
  30.3 103.0 %copy-start.5 = (f32[1024]{0:T(1024)S(1)}, f32[1024]{0:T(1024)}, u32[]{:S(2)}) copy-start(f32[1024]{0:T(1024)} %param.6) | copy-start | bytes 12292
  40.4 1.9 %copy-start = (bf16[1024,2048]{1,0:T(8,128)(2,1)}, bf16[1024,2048]{1,0:T(8,128)(2,1)S(1)}, u32[]{:S(2)}) copy-start(bf16[1024,2048]{1,0:T(8,128)(2,1)S(1)} %get-tuple-element.18) | copy-start | bytes 12582916
  133.3 14.7 %collective-permute-start = (bf16[64,2048]{1,0:T(8,128)(2,1)S(1)}, bf16[64,2048]{1,0:T(8,128)(2,1)}, u32[]{:S(2)}, u32[]{:S(2)}) collective-permute-start(bf16[64,2048]{1,0:T(8,128)(2,1)S(1)} %constant_dynamic-slice_fusion), channel_id=1, source_target_pairs={{0,1},{1,0},{2,3},{3,2},{4,5},{5,4},{6,7},{7,6},{8,9},{9,8},{10,11... | collective-permute-start | bytes 786440 | tf_op jit(solution)/shard_map/ppermute | solution.py:332
  152.7 3.5 %copy-start.6 = (f32[3,8,8,1024]{3,2,0,1:T(8,128)}, f32[3,8,8,1024]{3,2,0,1:T(8,128)S(1)}, u32[]{:S(2)}) copy-start(f32[3,8,8,1024]{3,2,0,1:T(8,128)S(1)} %copy.13) | copy-start | bytes 2359300
Sparse Core Ops, SparseCore 0:
  42.5 89.7 reduce-scatter.1

commit v2 on v1

v2 whole, which is shorter than its diff:
```python
import functools

import jax
import jax.numpy as jnp
import numpy as np
from jax import lax
from jax.experimental import pallas as pl
from jax.experimental.pallas import tpu as pltpu
from jax.sharding import Mesh, PartitionSpec as P

D = 1024
HEADS = 16
HEAD_DIM = 64
GROUP = 16
CLASSES = 8
BLOCK = 16
HALF = 512
SCALE = HEAD_DIM ** (-0.5)
EPS = 1e-05
BF = jnp.bfloat16
F32 = jnp.float32
MESH = pl.DeviceIdType.MESH
MB = 1024 * 1024


def dot(a, b, ca, cb):
    return lax.dot_general(a, b, (((ca,), (cb,)), ((), ())), preferred_element_type=F32)


def permutation(transposed):
    shape = (128, 128)
    r = lax.broadcasted_iota(jnp.int32, shape, 1 if transposed else 0)
    s = lax.broadcasted_iota(jnp.int32, shape, 0 if transposed else 1)
    a = 2 * ((r >> 3) & 1) + ((r >> 6) & 1)
    p = 2 * ((r >> 2) & 1) + ((r >> 5) & 1)
    c = 2 * (r & 3) + ((r >> 4) & 1)
    return jnp.where(s == (a * 4 + p) * 8 + c, 1.0, 0.0).astype(BF)


def place():
    core = lax.axis_index("core")
    chip = lax.axis_index("chip")
    base = (chip // CLASSES) * CLASSES
    mine = (chip - base) * 2 + core
    return core, chip, base, mine


def device(base, local):
    return {"chip": base + local // 2, "core": local % 2}


def enter(base, mine, low, high):
    barrier = pltpu.get_barrier_semaphore()

    def greet(j, _):
        pl.semaphore_signal(
            barrier, inc=1, device_id=device(base, lax.rem(mine + j, GROUP)), device_id_type=MESH
        )
        return 0

    lax.fori_loop(1, GROUP, greet, 0)
    pl.semaphore_wait(barrier, GROUP - 1)
    if high > 1 and low * high > CLASSES:
        chip = lax.axis_index("chip")
        level = chip // low
        for step, there in ((low, level < high - 1), (-low, level > 0)):

            @pl.when(there)
            def _():
                pl.semaphore_signal(
                    barrier, inc=1, device_id={"chip": chip + step}, device_id_type=MESH
                )

        for there in (level < high - 1, level > 0):

            @pl.when(there)
            def _():
                pl.semaphore_wait(barrier, 1)


def normalise(x):
    wide = x.astype(F32)
    centre = wide - jnp.mean(wide, axis=-1, keepdims=True)
    inverse = lax.rsqrt(jnp.mean(centre * centre, axis=-1, keepdims=True) + EPS)
    return centre * inverse, inverse


def vmem():
    return pl.BlockSpec(memory_space=pltpu.VMEM)


def chunk_of(kind, h):
    return h // 4 if kind == 3 else 2 + 3 * (h // 4) + kind


def kernel(
    low, high, tok, cot, gain, w_in, w_out, out, grad, gin, gout, gsum,
    ptok, pcot, x, g, wi, wo, nrm, proj, softs, feat, allf, alld, terms, inbox, outbox,
    part_out, part_dn, oland, dland, oret, dret, oin, din, fin, fland,
    wsem, gsend, grecv, psend, precv, fsend, frecv, dsend, drecv, zsend, zrecv, bsend, brecv,
):
    rows = D // (low * high)
    core, chip, base, mine = place()
    level, side = chip // low, lax.rem(chip, low)
    cols = pl.multiple_of(core * HALF, HALF)
    weights = [
        pltpu.make_async_copy(w_in.at[:, pl.ds(i * D + cols, HALF)], wi.at[i], wsem.at[i])
        for i in range(3)
    ]
    weights.append(pltpu.make_async_copy(w_out.at[pl.ds(cols, HALF), :], wo, wsem.at[3]))
    for c in weights:
        c.start()
    perm = permutation(False)
    ptok[...] = jnp.dot(perm, tok[...], preferred_element_type=F32).astype(BF)
    pcot[...] = jnp.dot(perm, cot[...], preferred_element_type=F32).astype(BF)
    enter(base, mine, low, high)

    def class_copy(k, src, dst, j):
        peer = lax.rem(mine + j, GROUP)
        there = pl.ds(pl.multiple_of((peer // 2) * BLOCK, BLOCK), BLOCK)
        span = pl.ds(pl.multiple_of((peer % 2) * HALF, HALF), HALF)
        landing = pl.ds(pl.multiple_of(mine * BLOCK, BLOCK), BLOCK)
        return pltpu.make_async_remote_copy(
            src_ref=src.at[there, span],
            dst_ref=dst.at[landing, span],
            send_sem=gsend.at[k, j],
            recv_sem=grecv.at[k, j],
            device_id=device(base, peer),
            device_id_type=MESH,
        )

    def partner(src, dst, slot):
        return pltpu.make_async_remote_copy(
            src_ref=src,
            dst_ref=dst,
            send_sem=psend.at[slot],
            recv_sem=precv.at[slot],
            device_id={"core": 1 - core},
            device_id_type=MESH,
        )

    def wait(c):
        c.wait_send()
        c.wait_recv()

    span = pl.ds(cols, HALF)
    own = pl.ds(pl.multiple_of(mine * BLOCK, BLOCK), BLOCK)
    own_class = pl.ds(pl.multiple_of((mine // 2) * BLOCK, BLOCK), BLOCK)
    pairs = ((ptok, x), (pcot, g))
    for k, (src, dst) in enumerate(pairs):

        def begin(j, _):
            class_copy(k, src, dst, j).start()
            return 0

        lax.fori_loop(1, GROUP, begin, 0)
        dst[own, span] = src[own_class, span]

    def arrived(k):
        src, dst = pairs[k]

        def finish(j, _):
            wait(class_copy(k, src, dst, j))
            return 0

        lax.fori_loop(1, GROUP, finish, 0)
        f = partner(dst.at[:, span], dst.at[:, span], k)
        f.start()
        return f

    def side_feature(k, j):
        peer = lax.rem(side + j, low)
        return pltpu.make_async_remote_copy(
            src_ref=feat.at[k, :, peer],
            dst_ref=allf.at[k, side],
            send_sem=fsend.at[k, j],
            recv_sem=frecv.at[k, j],
            device_id={"chip": chip - side + peer},
            device_id_type=MESH,
        )

    def side_chunk(c, j):
        peer = lax.rem(side + j, low)
        return pltpu.make_async_remote_copy(
            src_ref=alld.at[side, c],
            dst_ref=alld.at[side, c],
            send_sem=dsend.at[c, j],
            recv_sem=drecv.at[c, j],
            device_id={"chip": chip - side + peer},
            device_id_type=MESH,
        )

    def share_feature(k, turned):
        feat[k] = turned.reshape(high, low, rows, 256)
        for j in range(1, low):
            side_feature(k, j).start()
        allf[k, side] = feat[k, :, side]

    def share_chunk(c):
        for j in range(1, low):
            side_chunk(c, j).start()

    wait(arrived(0))
    standard, _ = normalise(x[...])
    scaled = standard * gain[...]
    nrm[...] = scaled.astype(BF)
    share_feature(0, scaled.T.astype(BF))
    for i in range(3):
        weights[i].wait()
        proj[i] = dot(nrm[...], wi[i], 1, 0).astype(BF)
    forward_g = arrived(1)

    heads = HALF // HEAD_DIM
    at = [slice(h * HEAD_DIM, (h + 1) * HEAD_DIM) for h in range(heads)]
    within = [slice((h % 4) * HEAD_DIM, (h % 4 + 1) * HEAD_DIM) for h in range(heads)]
    for h in range(heads):
        scores = dot(proj[0, :, at[h]], proj[1, :, at[h]], 1, 1) * SCALE
        shifted = jnp.exp(scores - jnp.max(scores, axis=-1, keepdims=True))
        soft = shifted / jnp.sum(shifted, axis=-1, keepdims=True)
        softs[h] = soft
        alld[side, chunk_of(3, h), :, within[h]] = dot(
            soft.astype(BF), proj[2, :, at[h]], 1, 0
        ).astype(BF)
        if h % 4 == 3:
            share_chunk(chunk_of(3, h))
    weights[3].wait()
    part_out[...] = dot(alld[side, 0], wo[:256, :], 1, 0) + dot(alld[side, 1], wo[256:, :], 1, 0)
    theirs = pl.ds(pl.multiple_of((1 - core) * 128, 128), 128)
    ours = pl.ds(pl.multiple_of(core * 128, 128), 128)
    swap_out = partner(part_out.at[theirs, :], oland, 2)
    swap_out.start()
    wait(forward_g)
    share_feature(1, g[...].astype(F32).T.astype(BF))
    proj[3] = dot(g[...], wo[...], 1, 1).astype(BF)

    def send_back(k, src, dst, j):
        landing = pl.ds(pl.multiple_of((mine // 2) * BLOCK, BLOCK), BLOCK)
        return pltpu.make_async_remote_copy(
            src_ref=src.at[j * BLOCK : (j + 1) * BLOCK, :],
            dst_ref=dst.at[landing, :],
            send_sem=bsend.at[k, j],
            recv_sem=brecv.at[k, mine // 2],
            device_id=device(base, core * 8 + j),
            device_id_type=MESH,
        )

    def deliver(k, src, dst):
        for j in range(8):

            @pl.when(core * 8 + j != mine)
            def _():
                send_back(k, src, dst, j).start()

            @pl.when(core * 8 + j == mine)
            def _():
                dst[own_class, :] = src[j * BLOCK : (j + 1) * BLOCK, :]

    wait(swap_out)
    oret[...] = (part_out[ours, :] + oland[...]).astype(BF)
    deliver(0, oret, oin)

    def backward(h):
        q, k, v, do = (proj[i, :, at[h]] for i in range(4))
        soft = softs[h]
        d_soft = dot(do, v, 1, 1)
        d_scores = soft * (d_soft - jnp.sum(soft * d_soft, axis=-1, keepdims=True))
        d_scaled = (d_scores * SCALE).astype(BF)
        w = within[h]
        alld[side, chunk_of(0, h), :, w] = dot(d_scaled, k, 1, 0).astype(BF)
        alld[side, chunk_of(1, h), :, w] = dot(d_scaled, q, 0, 0).astype(BF)
        alld[side, chunk_of(2, h), :, w] = dot(soft.astype(BF), do, 0, 0).astype(BF)
        if h % 4 == 3:
            for i in range(3):
                share_chunk(chunk_of(i, h))

    def line(way, t, c):
        return pltpu.make_async_remote_copy(
            src_ref=outbox.at[way, t, c],
            dst_ref=inbox.at[way, t, c],
            send_sem=zsend.at[way, t, c],
            recv_sem=zrecv.at[way, t, c],
            device_id={"chip": lax.rem(chip + (low if way == 0 else low * (high - 1)), low * high)},
            device_id_type=MESH,
        )

    def term(c):
        kind = jnp.where(c < 2, 1, 0)
        total = None
        for j in range(1, low):
            side_chunk(c, j).wait_recv()
        for s in range(low):
            part = dot(allf[kind, s].reshape(high * rows, 256), alld[s, c], 1, 0)
            total = part if total is None else total + part
        terms[c] = total.reshape(high, rows, 256)

    def relay(way, c):
        for t in range(high - 1, 0, -1) if way == 0 else range(high - 1):
            ahead = level < t if way == 0 else level > t
            first = level == (0 if way == 0 else high - 1)

            @pl.when(ahead & first)
            def _():
                outbox[way, t, c] = terms[c, t].astype(BF)
                line(way, t, c).start()

            @pl.when(ahead & jnp.logical_not(first))
            def _():
                line(way, t, c).wait_recv()
                outbox[way, t, c] = (terms[c, t] + inbox[way, t, c].astype(F32)).astype(BF)
                line(way, t, c).start()

    chunks = 8

    def step(s, fresh):
        if fresh:
            term(s)
        for way, lag in ((0, level), (1, high - 1 - level)):
            c = s - lag

            @pl.when((c >= 0) & (c < chunks))
            def _():
                relay(way, c)

    for h in range(4):
        backward(h)
    for k in range(2):
        for j in range(1, low):
            side_feature(k, j).wait_recv()
    step(0, True)
    for h in range(4, 8):
        backward(h)
    step(1, True)
    total = None
    for i in range(3):
        for half in range(2):
            part = dot(alld[side, 2 + 3 * half + i], wi[i, :, half * 256 : (half + 1) * 256], 1, 1)
            total = part if total is None else total + part
    part_dn[...] = total
    swap_dn = partner(part_dn.at[theirs, :], dland, 3)
    swap_dn.start()
    step(2, True)
    wait(swap_dn)
    standard, inverse = normalise(x[ours, :])
    weighted = (part_dn[ours, :] + dland[...]) * gain[...]
    mean_one = jnp.mean(weighted, axis=-1, keepdims=True)
    mean_two = jnp.mean(weighted * standard, axis=-1, keepdims=True)
    dret[...] = (inverse * (weighted - mean_one - standard * mean_two)).astype(BF)
    deliver(1, dret, din)

    def fresh_step(s, _):
        step(s, True)
        return 0

    def late_step(s, _):
        step(s, False)
        return 0

    lax.fori_loop(3, chunks, fresh_step, 0)
    lax.fori_loop(chunks, chunks + high - 1, late_step, 0)

    home = mine // 8
    inverse_perm = permutation(True)
    for k, (src, dst, result) in enumerate(((oret, oin, out), (dret, din, grad))):
        for j in range(8):

            @pl.when(core * 8 + j != mine)
            def _():
                send_back(k, src, dst, j).wait_send()

            @pl.when(j * 2 + home != mine)
            def _():
                pltpu.make_async_remote_copy(
                    src_ref=src.at[j * BLOCK : (j + 1) * BLOCK, :],
                    dst_ref=dst.at[j * BLOCK : (j + 1) * BLOCK, :],
                    send_sem=bsend.at[k, j],
                    recv_sem=brecv.at[k, j],
                    device_id={"core": 1 - core},
                    device_id_type=MESH,
                ).wait_recv()

        result[...] = jnp.dot(inverse_perm, dst[...], preferred_element_type=F32).astype(BF)

    w_rows = pl.ds(pl.multiple_of(chip * rows, rows), rows)
    gain_sum = jnp.zeros((rows, 1), F32)
    for c in range(chunks):
        span = slice(c * 256, (c + 1) * 256)
        fin[:, span] = terms[c, level]
        for way, there in ((0, level > 0), (1, level < high - 1)):

            @pl.when(there)
            def _():
                line(way, level, c).wait_recv()
                fin[:, span] += inbox[way, level, c].astype(F32)

        if c >= 2:
            half, i = divmod(c - 2, 3)
            w = wi[i, w_rows, half * 256 : (half + 1) * 256].astype(F32)
            gain_sum = gain_sum + jnp.sum(w * fin[:, span], axis=-1, keepdims=True)
    fin[:, chunks * 256 :] = jnp.broadcast_to(gain_sum, (rows, 128))
    few = rows // 2
    their_rows = pl.ds(pl.multiple_of((1 - core) * few, few), few)
    our_rows = pl.ds(pl.multiple_of(core * few, few), few)
    swap_fin = partner(fin.at[their_rows, :], fland, 4)
    swap_fin.start()

    def place_rows(who, values):
        for c in range(chunks):
            piece = values(slice(c * 256, (c + 1) * 256))
            if c < 2:
                gout[pl.ds(pl.multiple_of(who * HALF + c * 256, 256), 256), :] = piece.T
            else:
                half, i = divmod(c - 2, 3)
                where = pl.ds(pl.multiple_of(i * D + who * HALF + half * 256, 256), 256)
                gin[:, where] = piece

    place_rows(core, lambda s: fin[our_rows, s])
    wait(swap_fin)
    place_rows(1 - core, lambda s: fland[:, s])
    gsum[...] = fin[our_rows, chunks * 256 :] + fland[:, chunks * 256 :]

    for k in range(2):
        for j in range(1, low):
            side_feature(k, j).wait_send()

    def drain(c, _):
        for j in range(1, low):
            side_chunk(c, j).wait_send()
        for t in range(high):
            for way in range(2):
                sent = level < t if way == 0 else level > t

                @pl.when(sent)
                def _():
                    line(way, t, c).wait_send()

        return 0

    lax.fori_loop(0, chunks, drain, 0)


def per_device(tokens, norm_gain, in_projection, out_projection, out_cotangent):
    chips = lax.axis_size("chip")
    low = 1
    while 4 * low * low <= chips:
        low *= 2
    high = chips // low
    rows = D // chips
    few = rows // 2
    sems = pltpu.SemaphoreType.DMA
    layer_output, grad_tokens, grad_in, grad_out, gain_sum = pl.pallas_call(
        functools.partial(kernel, low, high),
        out_shape=[
            jax.ShapeDtypeStruct((128, D), BF),
            jax.ShapeDtypeStruct((128, D), BF),
            jax.ShapeDtypeStruct((few, 3 * D), F32),
            jax.ShapeDtypeStruct((D, few), F32),
            jax.ShapeDtypeStruct((few, 128), F32),
        ],
        in_specs=[vmem()] * 3 + [pl.BlockSpec(memory_space=pl.ANY)] * 2,
        out_specs=[vmem()] * 5,
        scratch_shapes=[
            pltpu.VMEM((128, D), BF),
            pltpu.VMEM((128, D), BF),
            pltpu.VMEM((256, D), BF),
            pltpu.VMEM((256, D), BF),
            pltpu.VMEM((3, D, HALF), BF),
            pltpu.VMEM((HALF, D), BF),
            pltpu.VMEM((256, D), BF),
            pltpu.VMEM((4, 256, HALF), BF),
            pltpu.VMEM((8, 256, 256), F32),
            pltpu.VMEM((2, high, low, rows, 256), BF),
            pltpu.VMEM((2, low, high, rows, 256), BF),
            pltpu.VMEM((low, 8, 256, 256), BF),
            pltpu.VMEM((8, high, rows, 256), F32),
            pltpu.VMEM((2, high, 8, rows, 256), BF),
            pltpu.VMEM((2, high, 8, rows, 256), BF),
            pltpu.VMEM((256, D), F32),
            pltpu.VMEM((256, D), F32),
            pltpu.VMEM((128, D), F32),
            pltpu.VMEM((128, D), F32),
            pltpu.VMEM((128, D), BF),
            pltpu.VMEM((128, D), BF),
            pltpu.VMEM((128, D), BF),
            pltpu.VMEM((128, D), BF),
            pltpu.VMEM((rows, 8 * 256 + 128), F32),
            pltpu.VMEM((few, 8 * 256 + 128), F32),
            sems((4,)),
            sems((2, GROUP)),
            sems((2, GROUP)),
            sems((5,)),
            sems((5,)),
            sems((2, low)),
            sems((2, low)),
            sems((8, low)),
            sems((8, low)),
            sems((2, high, 8)),
            sems((2, high, 8)),
            sems((2, 8)),
            sems((2, 8)),
        ],
        compiler_params=pltpu.CompilerParams(
            collective_id=0, has_side_effects=True, vmem_limit_bytes=56 * MB
        ),
    )(tokens, out_cotangent, norm_gain.reshape(1, D), in_projection, out_projection)
    start = (lax.axis_index("chip") * 2 + lax.axis_index("core")) * few
    my_gain = lax.dynamic_slice_in_dim(norm_gain, start, few, 0)
    return layer_output, grad_tokens, grad_in, grad_out, gain_sum[:, 0] / my_gain


def solution(mesh):
    parts, bricks = mesh.devices.shape
    fine = Mesh(mesh.devices.reshape(parts, bricks // 2, 2), ("parts", "chip", "core"))
    every = ("parts", "chip", "core")
    placed = (P(every, None), P(), P(), P(), P(every, None))
    return jax.shard_map(
        per_device,
        mesh=fine,
        in_specs=placed,
        out_specs=(
            P(every, None),
            P(every, None),
            P(every, None),
            P("parts", ("chip", "core")),
            P(every),
        ),
        check_vma=False,
    )
```

time: 165 us -> 100 us (0.61); the launches traced: 163 us -> 99.9 us
  waiting for transfers between devices: 90 us -> 0 us
  Pallas kernels: 43.5 us -> 89.8 us
  between operations: 14.2 us -> 0.65 us
  local copies, waits for them, and re-layouts: 11.8 us -> 8.19 us
  other arithmetic: 3.45 us -> 1.29 us
    reduce_scatter x1 -> x0, waiting for transfers between devices: 89.9 us -> none  [per_device(): summed = lax.psum_scatter(terms, 'chip', scatter_dimension=0, tiled=True)]
    pallas_call x3 -> x1, Pallas kernels: 43.5 us -> 89.8 us  [per_device(): pl.pallas_call(functools.partial(kernel, low, high), out_shape=[jax.Shape...]
    unnamed x17 -> x4, local copies, waits for them, and re-layouts: 7.59 us -> 7.33 us
  transfers between devices with their start and end apart: 2 -> 0, of which waited for: 1 -> 0; matrix products, arithmetic and copies ran while one was open for 0% -> 0% of each run, Pallas kernels for 9% -> 0%
where the time goes in v2:
time: 100 us; the launch traced here: 99.9 us
  Pallas kernels  89.8 us (90%)
  local copies, waits for them, and re-layouts  8.19 us (8%)
  other arithmetic  1.29 us (1%)
    pallas_call x1, Pallas kernels, per_device(): pl.pallas_call(functools.partial(kernel, low, high), out_shape=[jax.Shape...  89.8 us
    unnamed x4, local copies, waits for them, and re-layouts  7.33 us

profile of v2, /device:TPU:0, one launch (start us, length us, event | category | flops | bytes accessed | tf_op | source)
XLA Modules:
  0.0 99.9 jit_solution(2583258871275283382)
XLA Ops:
  0.6 89.8 %shard_map.92 = (bf16[128,1024]{1,0:T(8,128)(2,1)}, bf16[128,1024]{1,0:T(8,128)(2,1)}, f32[64,3072]{1,0:T(8,128)}, f32[1024,64]{1,0:T(8,128)}, f32[64,128]{1,0:T(8,128)}) custom-call(bf16[128,1024]{1,0:T(8,128)(2,1)} %tok.1, bf16[128,1024]{1,0:T(8,128)(2,1)} %cot.1, f32[1,1024]{1,0:T(1,128)} %bitcast.1, bf16[1024,3072]{1,0:T(8,128)(2,1)} %w_in.1, ...), custom_call_target="tpu_custom_call" | custom-call | tf_op jit(solution)/shard_map/pallas_call | solution.py:450
  90.4 0.9 slice_reduce_fusion
  91.3 1.3 %dynamic-slice_divide_fusion = f32[64]{0:T(128)} fusion(f32[64]{0:T(128)S(1)} %slice_reduce_fusion, f32[1024]{0:T(1024)} %param.6, s32[]{:T(128)S(6)} %select_n.3), kind=kLoop, calls=%fused_computation.1 | loop fusion | flops 64 | bytes 772 | tf_op jit(solution)/shard_map/div | solution.py:507
  92.6 1.9 %copy.11 = f32[1024,64]{0,1:T(8,128)} copy(f32[1024,64]{1,0:T(8,128)} %get-tuple-element.23) | data formatting | bytes 524288
  94.5 1.7 %copy.15 = bf16[128,1024]{1,0:T(8,128)(2,1)} copy(bf16[128,1024]{1,0:T(8,128)(2,1)} %get-tuple-element.30) | data formatting | bytes 524288
  96.2 1.7 %copy.16 = bf16[128,1024]{1,0:T(8,128)(2,1)} copy(bf16[128,1024]{1,0:T(8,128)(2,1)} %get-tuple-element.31) | data formatting | bytes 524288
  97.8 2.1 %copy.17 = f32[64,3072]{1,0:T(8,128)} copy(f32[64,3072]{1,0:T(8,128)} %get-tuple-element.32) | data formatting | bytes 1572864

commit v3 on v2

--- a/solution.py
+++ b/solution.py
@@ -396,7 +396,10 @@
             half, i = divmod(c - 2, 3)
             w = wi[i, w_rows, half * 256 : (half + 1) * 256].astype(F32)
             gain_sum = gain_sum + jnp.sum(w * fin[:, span], axis=-1, keepdims=True)
-    fin[:, chunks * 256 :] = jnp.broadcast_to(gain_sum, (rows, 128))
+    lane = lax.broadcasted_iota(jnp.int32, (rows, D), 1)
+    mine_lane = chip * rows + lax.broadcasted_iota(jnp.int32, (rows, D), 0)
+    my_gain = jnp.sum(jnp.where(lane == mine_lane, gain[...], 0.0), axis=-1, keepdims=True)
+    fin[:, chunks * 256 :] = jnp.broadcast_to(gain_sum / my_gain, (rows, 128))
     few = rows // 2
     their_rows = pl.ds(pl.multiple_of((1 - core) * few, few), few)
     our_rows = pl.ds(pl.multiple_of(core * few, few), few)
@@ -407,7 +410,7 @@
         for c in range(chunks):
             piece = values(slice(c * 256, (c + 1) * 256))
             if c < 2:
-                gout[pl.ds(pl.multiple_of(who * HALF + c * 256, 256), 256), :] = piece.T
+                gout[:, pl.ds(pl.multiple_of(who * HALF + c * 256, 256), 256)] = piece
             else:
                 half, i = divmod(c - 2, 3)
                 where = pl.ds(pl.multiple_of(i * D + who * HALF + half * 256, 256), 256)
@@ -416,7 +419,7 @@
     place_rows(core, lambda s: fin[our_rows, s])
     wait(swap_fin)
     place_rows(1 - core, lambda s: fland[:, s])
-    gsum[...] = fin[our_rows, chunks * 256 :] + fland[:, chunks * 256 :]
+    gsum[...] = (fin[our_rows, chunks * 256 :] + fland[:, chunks * 256 :]).T[:1, :]
 
     for k in range(2):
         for j in range(1, low):
@@ -436,6 +439,28 @@
         return 0
 
     lax.fori_loop(0, chunks, drain, 0)
+
+
+def settle_kernel(*refs):
+    sem = refs[-1]
+    half = (len(refs) - 1) // 2
+    copies = [pltpu.make_async_copy(refs[i], refs[half + i], sem.at[i]) for i in range(half)]
+    for c in copies:
+        c.start()
+    for c in copies:
+        c.wait()
+
+
+def settle(*arrays):
+    anywhere = [pl.BlockSpec(memory_space=pl.ANY)] * len(arrays)
+    return pl.pallas_call(
+        settle_kernel,
+        out_shape=[jax.ShapeDtypeStruct(a.shape, a.dtype) for a in arrays],
+        in_specs=anywhere,
+        out_specs=anywhere,
+        scratch_shapes=[pltpu.SemaphoreType.DMA((len(arrays),))],
+        compiler_params=pltpu.CompilerParams(vmem_limit_bytes=56 * MB),
+    )(*arrays)
 
 
 def per_device(tokens, norm_gain, in_projection, out_projection, out_cotangent):
@@ -453,8 +478,8 @@
             jax.ShapeDtypeStruct((128, D), BF),
             jax.ShapeDtypeStruct((128, D), BF),
             jax.ShapeDtypeStruct((few, 3 * D), F32),
-            jax.ShapeDtypeStruct((D, few), F32),
-            jax.ShapeDtypeStruct((few, 128), F32),
+            jax.ShapeDtypeStruct((few, D), F32),
+            jax.ShapeDtypeStruct((1, few), F32),
         ],
         in_specs=[vmem()] * 3 + [pl.BlockSpec(memory_space=pl.ANY)] * 2,
         out_specs=[vmem()] * 5,
@@ -502,9 +527,8 @@
             collective_id=0, has_side_effects=True, vmem_limit_bytes=56 * MB
         ),
     )(tokens, out_cotangent, norm_gain.reshape(1, D), in_projection, out_projection)
-    start = (lax.axis_index("chip") * 2 + lax.axis_index("core")) * few
-    my_gain = lax.dynamic_slice_in_dim(norm_gain, start, few, 0)
-    return layer_output, grad_tokens, grad_in, grad_out, gain_sum[:, 0] / my_gain
+    settled = settle(layer_output, grad_tokens, grad_in, grad_out, gain_sum)
+    return settled[0], settled[1], settled[2], settled[3].T, settled[4].reshape(few)
 
 
 def solution(mesh):

time: 100 us -> 139 us (1.39)
  Pallas kernels: 89.8 us -> 138 us
  local copies, waits for them, and re-layouts: 8.19 us -> 0 us
    pallas_call x0 -> x1, Pallas kernels: none -> 48.8 us  [settle(): pl.pallas_call(settle_kernel, out_shape=[jax.ShapeDtypeStruct(a.shape, a....]
    unnamed x4 -> x0, local copies, waits for them, and re-layouts: 7.33 us -> none
where the time goes in v3:
time: 139 us
  Pallas kernels  138 us (99%)
    pallas_call x1, Pallas kernels, per_device(): pl.pallas_call(functools.partial(kernel, low, high), out_shape=[jax.Shape...  89.7 us
    pallas_call x1, Pallas kernels, settle(): pl.pallas_call(settle_kernel, out_shape=[jax.ShapeDtypeStruct(a.shape, a....  48.8 us

profile of v3, /device:TPU:0, one launch (start us, length us, event | category | flops | bytes accessed | tf_op | source)
XLA Modules:
  0.0 139.1 jit_solution(9602323341007160225)
XLA Ops:
  0.6 89.7 %shard_map.92 = (bf16[128,1024]{1,0:T(8,128)(2,1)}, bf16[128,1024]{1,0:T(8,128)(2,1)}, f32[64,3072]{1,0:T(8,128)}, f32[64,1024]{1,0:T(8,128)}, f32[1,64]{1,0:T(1,128)}) custom-call(bf16[128,1024]{1,0:T(8,128)(2,1)} %tok.1, bf16[128,1024]{1,0:T(8,128)(2,1)} %cot.1, f32[1,1024]{1,0:T(1,128)} %bitcast.3, bf16[1024,3072]{1,0:T(8,128)(2,1)} %w_in.1, ...), custom_call_target="tpu_custom_call" | custom-call | tf_op jit(solution)/shard_map/pallas_call | solution.py:475
  90.3 48.8 %shard_map.93 = (bf16[128,1024]{1,0:T(8,128)(2,1)}, bf16[128,1024]{1,0:T(8,128)(2,1)}, f32[64,3072]{1,0:T(8,128)}, f32[64,1024]{1,0:T(8,128)}, f32[1,64]{1,0:T(1,128)}) custom-call(bf16[128,1024]{1,0:T(8,128)(2,1)} %get-tuple-element.15.refs_0_, bf16[128,1024]{1,0:T(8,128)(2,1)} %get-tuple-element.16.refs_1_, f32[64,3072]{1,0:T(8,128)} %get-tuple-element.17.refs_2_, ...), custom_call_target="tpu_custom_call" | custom-call | tf_op jit(solution)/shard_map/pallas_call | solution.py:456

commit v4 on v3

--- a/solution.py
+++ b/solution.py
@@ -453,13 +453,14 @@
 
 def settle(*arrays):
     anywhere = [pl.BlockSpec(memory_space=pl.ANY)] * len(arrays)
+    held = [vmem()] * len(arrays)
     return pl.pallas_call(
         settle_kernel,
         out_shape=[jax.ShapeDtypeStruct(a.shape, a.dtype) for a in arrays],
-        in_specs=anywhere,
+        in_specs=held,
         out_specs=anywhere,
         scratch_shapes=[pltpu.SemaphoreType.DMA((len(arrays),))],
-        compiler_params=pltpu.CompilerParams(vmem_limit_bytes=56 * MB),
+        compiler_params=pltpu.CompilerParams(vmem_limit_bytes=8 * MB),
     )(*arrays)
 
 

time: 139 us -> 96.4 us (0.69)
  Pallas kernels: 138 us -> 90.9 us
  local copies, waits for them, and re-layouts: 0 us -> 4.64 us
    pallas_call x1, Pallas kernels: 48.8 us -> 1.18 us  [settle(): pl.pallas_call(settle_kernel, out_shape=[jax.ShapeDtypeStruct(a.shape, a....]
    unnamed x0 -> x10, local copies, waits for them, and re-layouts: none -> 4.64 us
where the time goes in v4:
time: 96.4 us; the launch traced here: 96.1 us
  Pallas kernels  90.9 us (94%)
  local copies, waits for them, and re-layouts  4.64 us (5%)
    pallas_call x1, Pallas kernels, per_device(): pl.pallas_call(functools.partial(kernel, low, high), out_shape=[jax.Shape...  89.7 us
    unnamed x10, local copies, waits for them, and re-layouts  4.64 us

profile of v4, /device:TPU:0, one launch (start us, length us, event | category | flops | bytes accessed | tf_op | source)
XLA Modules:
  0.0 96.1 jit_solution(17599298676971791350)
XLA Ops:
  0.6 89.7 %shard_map.92 = (bf16[128,1024]{1,0:T(8,128)(2,1)}, bf16[128,1024]{1,0:T(8,128)(2,1)}, f32[64,3072]{1,0:T(8,128)}, f32[64,1024]{1,0:T(8,128)}, f32[1,64]{1,0:T(1,128)}) custom-call(bf16[128,1024]{1,0:T(8,128)(2,1)} %tok.1, bf16[128,1024]{1,0:T(8,128)(2,1)} %cot.1, f32[1,1024]{1,0:T(1,128)} %bitcast.3, bf16[1024,3072]{1,0:T(8,128)(2,1)} %w_in.1, ...), custom_call_target="tpu_custom_call" | custom-call | tf_op jit(solution)/shard_map/pallas_call | solution.py:476
  90.3 0.0 copy-start
  90.3 1.1 %copy-done = f32[64,3072]{1,0:T(8,128)S(1)} copy-done((f32[64,3072]{1,0:T(8,128)S(1)}, f32[64,3072]{1,0:T(8,128)}, u32[]{:S(2)}) %copy-start) | copy-done | bytes 786456
  91.5 0.0 copy-start.1
  91.5 0.9 copy-done.1
  92.4 0.0 copy-start.2
  92.4 0.9 copy-done.2
  93.4 0.0 copy-start.3
  93.4 0.9 copy-done.3
  94.3 0.0 copy-start.4
  94.3 0.7 copy-done.4
  95.0 1.2 %shard_map.93 = (bf16[128,1024]{1,0:T(8,128)(2,1)}, bf16[128,1024]{1,0:T(8,128)(2,1)}, f32[64,3072]{1,0:T(8,128)}, f32[64,1024]{1,0:T(8,128)}, f32[1,64]{1,0:T(1,128)}) custom-call(bf16[128,1024]{1,0:T(8,128)(2,1)S(1)} %copy-done.1, bf16[128,1024]{1,0:T(8,128)(2,1)S(1)} %copy-done.2, f32[64,3072]{1,0:T(8,128)S(1)} %copy-done, f32[64,1024]{1,0:T(8,128)S(1)} %copy-done.3, ...), custom_call_target="tpu_custom_call" | custom-call | tf_op jit(solution)/shard_map/pallas_call | solution.py:457
Async XLA Ops:
  90.3 1.1 %copy-start = (f32[64,3072]{1,0:T(8,128)S(1)}, f32[64,3072]{1,0:T(8,128)}, u32[]{:S(2)}) copy-start(f32[64,3072]{1,0:T(8,128)} %get-tuple-element.17.refs_2_) | copy-start | bytes 2359300
  91.5 0.9 copy-start.1
  92.4 0.9 copy-start.2
  93.4 0.9 copy-start.3
  94.3 0.7 copy-start.4
